TPU v7x, 32 devices: a whole 2x2x4 slice. The times are simulated.
32 devices in a mesh: freq: 8 (over z, y), tm: 4 (over x, core).
Axes of the slice: x: 2, y: 2, z: 4, core: 2. Of those that a mesh axis runs over, the one named last changes fastest.
Arguments:
- spectrogram: bfloat16 [4096, 2048], P('freq', 'tm'), may hold values from -6 to 6
- low_share: int32 [127], replicated, may hold values from 24 to 44
- jitter: int32 [254], replicated, may hold values from 0 to 63
Outputs:
- best: float32 [9, 2048], P(None, 'tm')
All inputs are finite; a program needn't handle non-finite values.
Results may differ from a plain program's by a relative error of at most 0.0003.
Values sent between devices are 32-bit elements; how exact they have to be, the bound alone decides.
A program may use at most 64 MiB of HBM per device.

v0:
```python
import math

import jax
import jax.numpy as jnp
from jax import lax
from jax.sharding import PartitionSpec as P

SUMMED = 32
WIDTHS = 9


def passed_along(block, axis, distance):
    devices = range(lax.axis_size(axis))
    route = [(i - distance, i) for i in devices if i - distance in devices]
    return lax.ppermute(block, axis, route)


def swapped(block, axis, apart):
    count = lax.axis_size(axis)
    route = []
    for low in range(count):
        high = low | 1 << apart
        if high != low and high < count:
            route += [(low, high), (high, low)]
    return lax.ppermute(block, axis, route)


def widen(trial_rows, fetch_width):
    if fetch_width == 0:
        return trial_rows
    span_time = trial_rows.shape[-1]
    hop_count = min(-(-fetch_width // span_time), lax.axis_size("tm") - 1)
    pieces = [trial_rows]
    fetched = 0
    for hop_index in range(1, hop_count + 1):
        taken_cols = min(span_time, fetch_width - fetched)
        arrived = passed_along(trial_rows[..., span_time - taken_cols :], "tm", hop_index)
        pieces.insert(0, arrived)
        fetched = fetched + taken_cols
    if fetched < fetch_width:
        pieces.insert(
            0, jnp.zeros(trial_rows.shape[:-1] + (fetch_width - fetched,), trial_rows.dtype)
        )
    return jnp.concatenate(pieces, axis=-1)


def align_pair(low_set, high_set, margin, need_now, fetch_width):
    if fetch_width == 0:
        return (low_set[..., need_now:], high_set, margin - need_now)
    high_set = widen(high_set, fetch_width)
    low_set = widen(low_set, fetch_width - need_now)
    return (low_set, high_set, fetch_width - need_now)


def delay_of(trial_ids, subband_ids, trial_count, low_share, jitter):
    all_trials = low_share.shape[0] + 1
    rate_rows = jnp.take(low_share, all_trials // trial_count - 1 + subband_ids)
    return (trial_ids * rate_rows + jnp.take(jitter, trial_count - 2 + trial_ids)) // 64


def merge_rows(low_rows, high_rows, shifts, need_now):
    offsets = need_now - shifts
    bit_count = max(need_now.bit_length(), 1)
    moved = high_rows
    for bit_index in range(bit_count):
        step_size = 2**bit_index
        cols = moved.shape[-1]
        selected = (offsets >> bit_index & 1)[:, None] == 1
        moved = jnp.where(selected, moved[:, step_size:], moved[:, : cols - step_size])
    return low_rows + moved


def shards(spectrogram, low_share, jitter):
    trial_dev = spectrogram.shape[0] // SUMMED
    span_time = spectrogram.shape[1]
    all_trials = low_share.shape[0] + 1
    freq_bits = lax.axis_size("freq").bit_length() - 1
    device = lax.axis_index("freq")
    local_counts = []
    trial_count = 2
    while trial_count <= trial_dev:
        local_counts.append(trial_count)
        trial_count = trial_count * 2
    cross_counts = [trial_dev * 2 ** (bit_index + 1) for bit_index in range(freq_bits)]
    need_list = [count_now - 1 for count_now in local_counts + cross_counts] + [
        2 ** (WIDTHS - 1) - 1
    ]
    fetch_plan = []
    margin = 0
    for position in range(len(need_list)):
        need_now = need_list[position]
        if margin >= need_now:
            fetch_plan.append(0)
            margin = margin - need_now
            continue
        fetch_width = need_now
        for later_need in need_list[position + 1 :]:
            if fetch_width + later_need > span_time:
                break
            fetch_width = fetch_width + later_need
        fetch_plan.append(fetch_width)
        margin = fetch_width - need_now
    states = jnp.sum(spectrogram.reshape(trial_dev, SUMMED, span_time), axis=1, dtype=jnp.float32)[
        :, None, :
    ]
    margin = 0
    section_index = 0
    for trial_count in local_counts:
        need_now = trial_count - 1
        groups = states.shape[0] // 2
        low_set, high_set, margin = align_pair(
            states[0::2], states[1::2], margin, need_now, fetch_plan[section_index]
        )
        low_rows = jnp.repeat(low_set, 2, axis=1).reshape(groups * trial_count, -1)
        high_rows = jnp.repeat(high_set, 2, axis=1).reshape(groups * trial_count, -1)
        trial_ids = jnp.tile(jnp.arange(trial_count, dtype=jnp.int32), groups)
        subband_ids = device * (trial_dev // trial_count) + jnp.repeat(
            jnp.arange(groups, dtype=jnp.int32), trial_count
        )
        shifts = delay_of(trial_ids, subband_ids, trial_count, low_share, jitter)
        states = merge_rows(low_rows, high_rows, shifts, need_now).reshape(groups, trial_count, -1)
        section_index = section_index + 1
    trial_rows = states[0]
    trial_ids = jnp.arange(trial_dev, dtype=jnp.int32)
    for bit_index in range(freq_bits):
        trial_count = cross_counts[bit_index]
        need_now = trial_count - 1
        partner = swapped(trial_rows, "freq", bit_index)
        upper_half = device >> bit_index & 1
        low_rows = jnp.where(upper_half == 1, partner, trial_rows)
        high_rows = jnp.where(upper_half == 1, trial_rows, partner)
        low_rows, high_rows, margin = align_pair(
            low_rows, high_rows, margin, need_now, fetch_plan[section_index]
        )
        trial_ids = 2 * trial_ids + upper_half
        shifts = delay_of(trial_ids, device >> bit_index + 1, trial_count, low_share, jitter)
        trial_rows = merge_rows(low_rows, high_rows, shifts, need_now)
        section_index = section_index + 1
    if fetch_plan[section_index] > 0:
        trial_rows = widen(trial_rows, fetch_plan[section_index])
    signal = trial_rows / math.sqrt(all_trials * SUMMED)
    peak_rows = []
    window_sum = signal
    width_now = 1
    for level_index in range(WIDTHS):
        length = window_sum.shape[1]
        peak_rows.append(
            jnp.max(window_sum[:, length - span_time :], axis=0) / math.sqrt(width_now)
        )
        if level_index + 1 < WIDTHS:
            window_sum = window_sum[:, width_now:] + window_sum[:, : length - width_now]
            width_now = width_now * 2
    local_best = jnp.stack(peak_rows)
    return lax.pmax(local_best, "freq")


def solution(mesh):
    placed = (P("freq", "tm"), P(), P())
    return jax.shard_map(
        shards, mesh=mesh, in_specs=placed, out_specs=P(None, "tm"), check_vma=False
    )
```

profile of v0, /device:TPU:0, one launch (start us, length us, event | category | flops | bytes accessed | tf_op | source)
XLA Modules:
  0.0 77.4 jit_solution(4977622499532197884)
XLA Ops:
  0.0 1.2 %convert_reduce_fusion = f32[16,512]{1,0:T(8,128)S(1)} fusion(bf16[512,512]{1,0:T(8,128)(2,1)} %param.7), kind=kLoop, calls=%fused_computation.11 | loop fusion | flops 516096 | bytes 557056 | tf_op jit(solution)/shard_map/reduce_sum | solution.py:103
  1.3 2.3 %collective-permute-start = (f32[8,1,501]{2,0,1:T(8,128)S(1)}, f32[8,1,501]{2,0,1:T(8,128)S(1)}, u32[]{:S(2)}, u32[]{:S(2)}) collective-permute-start(f32[8,1,501]{2,0,1:T(8,128)S(1)} %slice.422), channel_id=1, source_target_pairs={{0,1},{1,2},{2,3},{4,5},{5,6},{6,7},{8,9},{9,10},{10,11},{12,13},{... | collective-permute-start | bytes 48104 | tf_op jit(solution)/shard_map/ppermute | solution.py:15
  3.7 4.5 %collective-permute-start.1 = (f32[8,1,502]{2,0,1:T(8,128)S(1)}, f32[8,1,502]{2,0,1:T(8,128)S(1)}, u32[]{:S(2)}, u32[]{:S(2)}) collective-permute-start(f32[8,1,502]{2,0,1:T(8,128)S(1)} %slice.423), channel_id=1, source_target_pairs={{0,1},{1,2},{2,3},{4,5},{5,6},{6,7},{8,9},{9,10},{10,11},{12,13},{... | collective-permute-start | bytes 48200 | tf_op jit(solution)/shard_map/ppermute | solution.py:15
  8.4 0.1 add.182
  8.5 0.6 copy-done.1
  9.0 0.7 fusion.34
  9.7 0.7 gather_fusion
  10.4 0.1 tile.42
  10.5 0.7 gather_fusion.1
  11.2 0.7 gather_fusion.3
  11.8 0.1 add.188
  11.9 0.7 gather_fusion.2
  12.6 0.1 tile.44
  12.7 0.7 gather_fusion.5
  13.4 0.1 add.195
  13.5 0.7 gather_fusion.4
  14.2 0.7 gather_fusion.7
  14.9 0.7 gather_fusion.6
  15.6 0.7 gather_fusion.8
  16.3 0.7 gather_fusion.10
  17.0 0.7 gather_fusion.9
  20.0 0.1 fusion.4
  20.2 0.1 slice.426
  20.4 0.1 slice_select_fusion.19
  20.5 0.1 fusion.3
  20.9 0.1 slice_select_fusion.17
  21.0 0.1 slice_select_fusion.16
  21.1 0.1 fusion.2
  21.5 0.1 slice_select_fusion.14
  21.6 0.1 slice_select_fusion.13
  21.7 0.1 slice_select_fusion.12
  21.8 0.1 fusion.1
  21.8 1.6 %collective-permute-start.2 = (f32[16,988]{1,0:T(8,128)S(1)}, f32[16,988]{1,0:T(8,128)S(1)}, u32[]{:S(2)}, u32[]{:S(2)}) collective-permute-start(f32[16,988]{1,0:T(8,128)S(1)} %fusion.1), channel_id=1, source_target_pairs={{0,4},{4,0},{8,12},{12,8},{16,20},{20,16},{24,28},{28,24},{1,5},{5... | collective-permute-start | bytes 189704 | tf_op jit(solution)/shard_map/ppermute | solution.py:25
  23.4 2.7 %collective-permute-done.2 = f32[16,988]{1,0:T(8,128)S(1)} collective-permute-done((f32[16,988]{1,0:T(8,128)S(1)}, f32[16,988]{1,0:T(8,128)S(1)}, u32[]{:S(2)}, u32[]{:S(2)}) %collective-permute-start.2) | collective-permute-done | bytes 63264 | tf_op jit(solution)/shard_map/ppermute | solution.py:25
  26.2 0.1 slice_select_fusion.9
  26.3 0.1 slice_select_fusion.8
  26.4 0.1 slice_select_fusion.7
  26.5 0.1 slice_select_fusion.6
  26.6 0.1 fusion
  26.7 1.6 %collective-permute-start.3 = (f32[16,957]{1,0:T(8,128)S(1)}, f32[16,957]{1,0:T(8,128)S(1)}, u32[]{:S(2)}, u32[]{:S(2)}) collective-permute-start(f32[16,957]{1,0:T(8,128)S(1)} %fusion), channel_id=1, source_target_pairs={{0,8},{8,0},{4,12},{12,4},{16,24},{24,16},{20,28},{28,20},{1,9},{9... | collective-permute-start | bytes 183752 | tf_op jit(solution)/shard_map/ppermute | solution.py:25
  28.3 2.7 %collective-permute-done.3 = f32[16,957]{1,0:T(8,128)S(1)} collective-permute-done((f32[16,957]{1,0:T(8,128)S(1)}, f32[16,957]{1,0:T(8,128)S(1)}, u32[]{:S(2)}, u32[]{:S(2)}) %collective-permute-start.3) | collective-permute-done | bytes 61280 | tf_op jit(solution)/shard_map/ppermute | solution.py:25
  31.0 0.1 slice_select_fusion.4
  31.1 0.1 slice_select_fusion.3
  31.2 0.1 slice_select_fusion.2
  31.3 0.1 slice_select_fusion.1
  31.4 0.1 slice_select_fusion
  31.5 0.1 fusion.5
  31.6 2.7 %collective-permute-start.4 = (f32[16,894]{1,0:T(8,128)S(1)}, f32[16,894]{1,0:T(8,128)S(1)}, u32[]{:S(2)}, u32[]{:S(2)}) collective-permute-start(f32[16,894]{1,0:T(8,128)S(1)} %fusion.5), channel_id=1, source_target_pairs={{0,16},{16,0},{4,20},{20,4},{8,24},{24,8},{12,28},{28,12},{1,17},{... | collective-permute-start | bytes 171656 | tf_op jit(solution)/shard_map/ppermute | solution.py:25
  34.3 2.5 %collective-permute-done.4 = f32[16,894]{1,0:T(8,128)S(1)} collective-permute-done((f32[16,894]{1,0:T(8,128)S(1)}, f32[16,894]{1,0:T(8,128)S(1)}, u32[]{:S(2)}, u32[]{:S(2)}) %collective-permute-start.4) | collective-permute-done | bytes 57248 | tf_op jit(solution)/shard_map/ppermute | solution.py:25
  36.8 0.1 slice_select_fusion.26
  36.9 0.1 slice_select_fusion.25
  37.0 0.1 slice_select_fusion.24
  37.1 0.1 slice_select_fusion.23
  37.2 0.1 slice_select_fusion.22
  37.2 0.1 slice_select_fusion.21
  37.3 0.1 fusion.7
  37.5 0.1 slice_reduce_fusion.6
  37.6 0.1 slice_reduce_fusion.5
  37.8 0.1 slice_reduce_fusion.4
  38.0 0.1 slice_reduce_fusion.3
  38.2 0.1 slice_reduce_fusion.2
  38.3 0.1 slice_reduce_fusion.1
  38.5 0.1 slice_reduce_fusion
  38.9 38.5 %pmax.7 = f32[9,512]{1,0:T(8,128)} all-reduce(f32[9,512]{1,0:T(8,128)S(1)} %stack.5), channel_id=1, replica_groups=mesh['freq'=8,'tm'=4] {'freq'}, use_global_device_ids=true, to_apply=%region_10.13 | all-reduce | flops 4608 | bytes 36864 | tf_op jit(solution)/shard_map/pmax | solution.py:154
  (94 shorter events, 2.3 us)
Async XLA Ops:
  0.0 10.5 %copy-start = (s32[254]{0:T(256)S(1)}, s32[254]{0:T(256)}, u32[]{:S(2)}) copy-start(s32[254]{0:T(256)} %param.9) | copy-start | bytes 3052
  1.3 18.4 %collective-permute-start = (f32[8,1,501]{2,0,1:T(8,128)S(1)}, f32[8,1,501]{2,0,1:T(8,128)S(1)}, u32[]{:S(2)}, u32[]{:S(2)}) collective-permute-start(f32[8,1,501]{2,0,1:T(8,128)S(1)} %slice.422), channel_id=1, source_target_pairs={{0,1},{1,2},{2,3},{4,5},{5,6},{6,7},{8,9},{9,10},{10,11},{12,13},{... | collective-permute-start | bytes 48104 | tf_op jit(solution)/shard_map/ppermute | solution.py:15
  3.7 16.1 %collective-permute-start.1 = (f32[8,1,502]{2,0,1:T(8,128)S(1)}, f32[8,1,502]{2,0,1:T(8,128)S(1)}, u32[]{:S(2)}, u32[]{:S(2)}) collective-permute-start(f32[8,1,502]{2,0,1:T(8,128)S(1)} %slice.423), channel_id=1, source_target_pairs={{0,1},{1,2},{2,3},{4,5},{5,6},{6,7},{8,9},{9,10},{10,11},{12,13},{... | collective-permute-start | bytes 48200 | tf_op jit(solution)/shard_map/ppermute | solution.py:15
  8.4 0.7 copy-start.1
  21.8 4.3 %collective-permute-start.2 = (f32[16,988]{1,0:T(8,128)S(1)}, f32[16,988]{1,0:T(8,128)S(1)}, u32[]{:S(2)}, u32[]{:S(2)}) collective-permute-start(f32[16,988]{1,0:T(8,128)S(1)} %fusion.1), channel_id=1, source_target_pairs={{0,4},{4,0},{8,12},{12,8},{16,20},{20,16},{24,28},{28,24},{1,5},{5... | collective-permute-start | bytes 189704 | tf_op jit(solution)/shard_map/ppermute | solution.py:25
  26.7 4.3 %collective-permute-start.3 = (f32[16,957]{1,0:T(8,128)S(1)}, f32[16,957]{1,0:T(8,128)S(1)}, u32[]{:S(2)}, u32[]{:S(2)}) collective-permute-start(f32[16,957]{1,0:T(8,128)S(1)} %fusion), channel_id=1, source_target_pairs={{0,8},{8,0},{4,12},{12,4},{16,24},{24,16},{20,28},{28,20},{1,9},{9... | collective-permute-start | bytes 183752 | tf_op jit(solution)/shard_map/ppermute | solution.py:25
  31.6 5.1 %collective-permute-start.4 = (f32[16,894]{1,0:T(8,128)S(1)}, f32[16,894]{1,0:T(8,128)S(1)}, u32[]{:S(2)}, u32[]{:S(2)}) collective-permute-start(f32[16,894]{1,0:T(8,128)S(1)} %fusion.5), channel_id=1, source_target_pairs={{0,16},{16,0},{4,20},{20,4},{8,24},{24,8},{12,28},{28,12},{1,17},{... | collective-permute-start | bytes 171656 | tf_op jit(solution)/shard_map/ppermute | solution.py:25
where the time goes:
time: 77.6 us; the launch traced here: 77.4 us
  blocking collectives  38.5 us (50%)
  starting transfers between devices  12.7 us (16%)
  local copies, waits for them, and re-layouts  10.1 us (13%)
  waiting for transfers between devices  7.9 us (10%)
  other arithmetic  5.41 us (7%)
  between operations  2.67 us (3%)
    pmax x1, blocking collectives, shards(): return lax.pmax(local_best, 'freq')  38.5 us
    ppermute x3, waiting for transfers between devices, swapped(): return lax.ppermute(block, axis, route)  7.89 us
    ppermute x2, starting transfers between devices, passed_along(): return lax.ppermute(block, axis, route)  6.85 us
    ppermute x3, starting transfers between devices, swapped(): return lax.ppermute(block, axis, route)  5.88 us
    gather x7, local copies, waits for them, and re-layouts, delay_of(): jnp.take(jitter, trial_count - 2 + trial_ids)  4.66 us
    gather x4, local copies, waits for them, and re-layouts, delay_of(): rate_rows = jnp.take(low_share, all_trials // trial_count - 1 + subband_ids)  2.63 us
    select_n x21, other arithmetic, merge_rows(): jnp.where(selected, moved[:, step_size:], moved[:, :cols - step_size])  1.79 us
  transfers between devices with their start and end apart: 5, of which 3 were waited for; matrix products, arithmetic and copies ran while one was open for 12% of the time, Pallas kernels for 0%

commit v1 on v0

--- a/solution.py
+++ b/solution.py
@@ -1,12 +1,18 @@
+import functools
 import math
 
 import jax
 import jax.numpy as jnp
 from jax import lax
+from jax.experimental import pallas as pl
+from jax.experimental.pallas import tpu as pltpu
 from jax.sharding import PartitionSpec as P
 
 SUMMED = 32
 WIDTHS = 9
+LANES = 128
+SUBLANES = 8
+MESH = pl.DeviceIdType.MESH
 
 
 def passed_along(block, axis, distance):
@@ -70,7 +76,7 @@
     return low_rows + moved
 
 
-def shards(spectrogram, low_share, jitter):
+def shards_any_reach(spectrogram, low_share, jitter):
     trial_dev = spectrogram.shape[0] // SUMMED
     span_time = spectrogram.shape[1]
     all_trials = low_share.shape[0] + 1
@@ -154,8 +160,273 @@
     return lax.pmax(local_best, "freq")
 
 
+def moved(row, above, delay, lane):
+    return pltpu.roll(jnp.where(lane >= LANES - delay, above, row), delay, 1)
+
+
+def merged(old, count, first_trial, first_subband, all_trials, share, rest, lane):
+    new = []
+    for s in range(len(old) // 2):
+        rate = share[all_trials // count - 1 + first_subband + s]
+        highs = [(row, pltpu.roll(row, 1, 0)) for row in old[2 * s + 1]]
+        trials = []
+        for j in range(2 * len(highs)):
+            trial = first_trial + j
+            delay = (trial * rate + rest[count - 2 + trial]) >> 6
+            trials.append(old[2 * s][j // 2] + moved(*highs[j // 2], delay, lane))
+        new.append(trials)
+    return new
+
+
+def search(
+    bands, slots, all_trials,
+    spec_hbm, share_hbm, rest_hbm, best_ref,
+    spec, share, rest, base_rows, rows, here, before, part, parts, mine, whole,
+    in_sem, here_send, here_recv, next_send, next_recv, part_send, part_recv, all_send, all_recv,
+):
+    k, m = lax.axis_index("freq"), lax.axis_index("tm")
+    span = spec.shape[1]
+    chunks = span // LANES
+    local = spec.shape[0] // SUMMED
+    each = local // bands
+
+    loads = [
+        pltpu.make_async_copy(spec_hbm, spec, in_sem.at[0]),
+        pltpu.make_async_copy(share_hbm, share, in_sem.at[1]),
+        pltpu.make_async_copy(rest_hbm, rest, in_sem.at[2]),
+    ]
+    for load in loads:
+        load.start()
+
+    barrier = pltpu.get_barrier_semaphore()
+    for j in range(1, bands):
+        pl.semaphore_signal(
+            barrier, inc=1, device_id=(lax.rem(k + j, bands), m), device_id_type=MESH
+        )
+
+    @pl.when(m > 0)
+    def _():
+        for j in range(bands):
+            pl.semaphore_signal(
+                barrier, inc=1, device_id=(lax.rem(k + j, bands), m - 1), device_id_type=MESH
+            )
+
+    lane = lax.broadcasted_iota(jnp.int32, (SUBLANES, LANES), 1)
+    base_rows[...] = jnp.zeros_like(base_rows)
+
+    @pl.when(m == 0)
+    def _():
+        before[...] = jnp.zeros_like(before)
+
+    for load in loads:
+        load.wait()
+
+    row_of = lax.broadcasted_iota(jnp.int32, (local, local * SUMMED), 0)
+    channel = lax.broadcasted_iota(jnp.int32, (local, local * SUMMED), 1)
+    ones = jnp.where(channel // SUMMED == row_of, 1.0, 0.0).astype(jnp.bfloat16)
+    base = jnp.dot(ones, spec[...], preferred_element_type=jnp.float32)
+    for q in range(chunks):
+        base_rows[:, q, :] = base[:, q * LANES : (q + 1) * LANES]
+    state = [[base_rows[s]] for s in range(local)]
+    count = 2
+    while count <= local:
+        state = merged(state, count, 0, k * (local // count), all_trials, share, rest, lane)
+        count = count * 2
+    for d in range(local):
+        rows[d] = state[0][d][: chunks + 1]
+
+    @pl.when(m < slots - 1)
+    def _():
+        pl.semaphore_wait(barrier, 2 * bands - 1)
+
+    @pl.when(m == slots - 1)
+    def _():
+        pl.semaphore_wait(barrier, bands - 1)
+
+    def here_copy(j):
+        to = lax.rem(k + j, bands)
+        return pltpu.make_async_remote_copy(
+            src_ref=rows.at[pl.ds(to * each, each)], dst_ref=here.at[k],
+            send_sem=here_send.at[j], recv_sem=here_recv.at[j],
+            device_id=(to, m), device_id_type=MESH,
+        )
+
+    def next_copy(j):
+        to = lax.rem(k + j, bands)
+        return pltpu.make_async_remote_copy(
+            src_ref=rows.at[pl.ds(to * each, each)], dst_ref=before.at[k],
+            send_sem=next_send.at[j], recv_sem=next_recv.at[j],
+            device_id=(to, m + 1), device_id_type=MESH,
+        )
+
+    def arrival(buffer, sems, j):
+        came = buffer.at[lax.rem(k + bands - j, bands)]
+        return pltpu.make_async_remote_copy(
+            src_ref=came, dst_ref=came, send_sem=sems.at[j], recv_sem=sems.at[j],
+            device_id=(k, m), device_id_type=MESH,
+        )
+
+    order = sorted(range(bands), key=lambda j: -min(j, bands - j))
+
+    @pl.when(m < slots - 1)
+    def _():
+        for j in order:
+            next_copy(j).start()
+
+    for j in order:
+        if j > 0:
+            here_copy(j).start()
+    here[k] = rows[pl.ds(k * each, each)]
+
+    for j in range(1, bands):
+        arrival(here, here_recv, j).wait_recv()
+
+    @pl.when(m > 0)
+    def _():
+        for j in range(bands):
+            arrival(before, next_recv, j).wait_recv()
+
+    state = []
+    for s in range(bands):
+        trials = []
+        for i in range(each):
+            own, old = here[s, i], before[s, i]
+            joint = own[:1] + old[chunks:]
+            trials.append(jnp.concatenate([old[:chunks], joint, own[1:chunks]], axis=0))
+        state.append(trials)
+    width = each
+    while count <= all_trials:
+        width = width * 2
+        state = merged(state, count, k * width, 0, all_trials, share, rest, lane)
+        count = count * 2
+
+    window = state[0]
+    flat = 0
+    piece = part.shape[1]
+    for level in range(WIDTHS):
+        w = 2**level
+        peak = functools.reduce(jnp.maximum, window)[chunks:]
+        peak = peak * (1.0 / math.sqrt(all_trials * SUMMED * w))
+        done = 0
+        while done < chunks:
+            slot = flat % piece
+            take = min(chunks - done, piece - slot)
+            part[flat // piece, slot : slot + take, :] = peak[done : done + take]
+            done, flat = done + take, flat + take
+        if level + 1 < WIDTHS:
+            later = []
+            for row in window:
+                above = pltpu.roll(row, 1, 0)
+                if w < LANES:
+                    above = moved(row, above, w, lane)
+                later.append(row + above)
+            window = later
+    while flat < bands * piece:
+        part[flat // piece, flat % piece : flat % piece + 1, :] = jnp.zeros((1, LANES), jnp.float32)
+        flat = flat + 1
+
+    def part_copy(j):
+        to = lax.rem(k + j, bands)
+        return pltpu.make_async_remote_copy(
+            src_ref=part.at[to], dst_ref=parts.at[k],
+            send_sem=part_send.at[j], recv_sem=part_recv.at[j],
+            device_id=(to, m), device_id_type=MESH,
+        )
+
+    def whole_copy(j):
+        to = lax.rem(k + j, bands)
+        return pltpu.make_async_remote_copy(
+            src_ref=mine, dst_ref=whole.at[k],
+            send_sem=all_send.at[j], recv_sem=all_recv.at[j],
+            device_id=(to, m), device_id_type=MESH,
+        )
+
+    for j in order:
+        if j > 0:
+            part_copy(j).start()
+    parts[k] = part[k]
+    for j in range(1, bands):
+        arrival(parts, part_recv, j).wait_recv()
+    mine[...] = functools.reduce(jnp.maximum, [parts[s] for s in range(bands)])
+    for j in order:
+        if j > 0:
+            whole_copy(j).start()
+    whole[k] = mine[...]
+    for j in range(1, bands):
+        here_copy(j).wait_send()
+        part_copy(j).wait_send()
+
+    @pl.when(m < slots - 1)
+    def _():
+        for j in range(bands):
+            next_copy(j).wait_send()
+
+    for j in range(1, bands):
+        arrival(whole, all_recv, j).wait_recv()
+    for flat in range(WIDTHS * chunks):
+        at = flat % chunks * LANES
+        best_ref[flat // chunks : flat // chunks + 1, at : at + LANES] = whole[
+            flat // piece, flat % piece : flat % piece + 1, :
+        ]
+    for j in range(1, bands):
+        whole_copy(j).wait_send()
+
+
+def one_block_back(mesh, channels, span, all_trials):
+    bands = mesh.shape["freq"]
+    local = channels // bands // SUMMED
+    if span * 2 != SUBLANES * LANES or all_trials > LANES or local % bands != 0:
+        return False
+    reach = sum(2**level - 1 for level in range(1, all_trials.bit_length()))
+    return reach + 2 ** (WIDTHS - 1) - 1 <= span
+
+
+def shards_one_back(bands, slots, spectrogram, low_share, jitter):
+    depth, span = spectrogram.shape
+    all_trials = low_share.shape[0] + 1
+    local = depth // SUMMED
+    chunks = span // LANES
+    each = local // bands
+    piece = -(-WIDTHS * chunks // bands)
+    sems = pltpu.SemaphoreType.DMA((bands,))
+    vmem = lambda *shape: pltpu.VMEM(shape, jnp.float32)
+    return pl.pallas_call(
+        functools.partial(search, bands, slots, all_trials),
+        out_shape=jax.ShapeDtypeStruct((WIDTHS, span), jnp.float32),
+        in_specs=[pl.BlockSpec(memory_space=pl.ANY)] * 3,
+        out_specs=pl.BlockSpec(memory_space=pltpu.VMEM),
+        scratch_shapes=[
+            pltpu.VMEM((depth, span), spectrogram.dtype),
+            pltpu.SMEM(low_share.shape, jnp.int32),
+            pltpu.SMEM(jitter.shape, jnp.int32),
+            vmem(local, SUBLANES, LANES),
+            vmem(local, chunks + 1, LANES),
+            vmem(bands, each, chunks + 1, LANES),
+            vmem(bands, each, chunks + 1, LANES),
+            vmem(bands, piece, LANES),
+            vmem(bands, piece, LANES),
+            vmem(piece, LANES),
+            vmem(bands, piece, LANES),
+            pltpu.SemaphoreType.DMA((3,)),
+        ]
+        + [sems] * 8,
+        compiler_params=pltpu.CompilerParams(
+            collective_id=0, has_side_effects=True, vmem_limit_bytes=16 * 2**20
+        ),
+    )(spectrogram, low_share, jitter)
+
+
 def solution(mesh):
     placed = (P("freq", "tm"), P(), P())
-    return jax.shard_map(
-        shards, mesh=mesh, in_specs=placed, out_specs=P(None, "tm"), check_vma=False
-    )
+    bands, slots = mesh.shape["freq"], mesh.shape["tm"]
+
+    def run(spectrogram, low_share, jitter):
+        channels, time = spectrogram.shape
+        body = shards_any_reach
+        if one_block_back(mesh, channels, time // slots, low_share.shape[0] + 1):
+            body = functools.partial(shards_one_back, bands, slots)
+        return jax.shard_map(
+            body, mesh=mesh, in_specs=placed, out_specs=P(None, "tm"), check_vma=False
+        )(spectrogram, low_share, jitter)
+
+    return run

time: 77.6 us -> 22.6 us (0.29)
  blocking collectives: 38.5 us -> 0 us
  Pallas kernels: 0 us -> 19.4 us
  starting transfers between devices: 12.7 us -> 0 us
  waiting for transfers between devices: 7.9 us -> 0 us
  local copies, waits for them, and re-layouts: 10.1 us -> 2.99 us
  other arithmetic: 5.41 us -> 0 us
  between operations: 2.67 us -> 0.01 us
    pmax x1 -> x0, blocking collectives: 38.5 us -> none  [shards(): return lax.pmax(local_best, 'freq')]
    pallas_call x0 -> x1, Pallas kernels: none -> 19.4 us  [shards_one_back(): pl.pallas_call(functools.partial(search, bands, slots, all_trials), out_s...]
    ppermute x5 -> x0, starting transfers between devices: 12.7 us -> none  [the longest x2 6.85 us: passed_along(): return lax.ppermute(block, axis, route)]
    ppermute x5 -> x0, waiting for transfers between devices: 7.9 us -> none  [the longest x3 7.89 us: swapped(): return lax.ppermute(block, axis, route)]
    gather x11 -> x0, local copies, waits for them, and re-layouts: 7.29 us -> none  [the longest x7 4.66 us: delay_of(): jnp.take(jitter, trial_count - 2 + trial_ids)]
    unnamed x4 -> x7, local copies, waits for them, and re-layouts: 0.56 us -> 2.99 us
    select_n x34 -> x0, other arithmetic: 1.89 us -> none  [the longest x21 1.79 us: merge_rows(): jnp.where(selected, moved[:, step_size:], moved[:, :cols - step_size])]
    another operation x15 -> x0, local copies, waits for them, and re-layouts: 1.26 us -> none  [the longest x2 0.67 us: delay_of(): rate_rows = jnp.take(low_share, all_trials // trial_count - 1 + subband_ids)]
  transfers between devices with their start and end apart: 5 -> 0, of which waited for: 3 -> 0; matrix products, arithmetic and copies ran while one was open for 12% -> 0% of each run, Pallas kernels for 0% -> 0%
where the time goes in v1:
time: 22.6 us; the launch traced here: 22.4 us
  Pallas kernels  19.4 us (86%)
  local copies, waits for them, and re-layouts  2.99 us (13%)
    pallas_call x1, Pallas kernels, shards_one_back(): pl.pallas_call(functools.partial(search, bands, slots, all_trials), out_s...  19.4 us
    unnamed x7, local copies, waits for them, and re-layouts  2.99 us

profile of v1, /device:TPU:0, one launch (start us, length us, event | category | flops | bytes accessed | tf_op | source)
XLA Modules:
  0.0 22.4 jit_solution(6893195030392570494)
XLA Ops:
  0.0 0.0 copy-start
  0.0 1.0 %copy-done = bf16[512,512]{1,0:T(8,128)(2,1)S(1)} copy-done((bf16[512,512]{1,0:T(8,128)(2,1)S(1)}, bf16[512,512]{1,0:T(8,128)(2,1)}, u32[]{:S(2)}) %copy-start) | copy-done | bytes 524312
  1.0 0.0 copy-start.1
  1.0 0.7 %copy-done.1 = s32[254]{0:T(256)S(1)} copy-done((s32[254]{0:T(256)S(1)}, s32[254]{0:T(256)}, u32[]{:S(2)}) %copy-start.1) | copy-done | bytes 1040
  1.7 0.0 copy-start.2
  1.7 0.7 %copy-done.2 = s32[127]{0:T(128)S(1)} copy-done((s32[127]{0:T(128)S(1)}, s32[127]{0:T(128)}, u32[]{:S(2)}) %copy-start.2) | copy-done | bytes 532
  2.4 19.4 %shard_map.37 = f32[9,512]{1,0:T(8,128)S(1)} custom-call(bf16[512,512]{1,0:T(8,128)(2,1)S(1)} %copy-done, s32[127]{0:T(128)S(1)} %copy-done.2, s32[254]{0:T(256)S(1)} %copy-done.1), custom_call_target="tpu_custom_call" | custom-call | tf_op jit(solution)/shard_map/pallas_call | solution.py:393
  21.8 0.6 %copy.5 = f32[9,512]{1,0:T(8,128)} copy(f32[9,512]{1,0:T(8,128)S(1)} %shard_map.37) | data formatting | bytes 36864
Async XLA Ops:
  0.0 1.0 %copy-start = (bf16[512,512]{1,0:T(8,128)(2,1)S(1)}, bf16[512,512]{1,0:T(8,128)(2,1)}, u32[]{:S(2)}) copy-start(bf16[512,512]{1,0:T(8,128)(2,1)} %spec_hbm.1) | copy-start | bytes 1572868
  1.0 0.7 %copy-start.1 = (s32[254]{0:T(256)S(1)}, s32[254]{0:T(256)}, u32[]{:S(2)}) copy-start(s32[254]{0:T(256)} %rest_hbm.1) | copy-start | bytes 3052
  1.7 0.7 %copy-start.2 = (s32[127]{0:T(128)S(1)}, s32[127]{0:T(128)}, u32[]{:S(2)}) copy-start(s32[127]{0:T(128)} %share_hbm.1) | copy-start | bytes 1528

commit v2 on v1

--- a/solution.py
+++ b/solution.py
@@ -393,7 +393,7 @@
     return pl.pallas_call(
         functools.partial(search, bands, slots, all_trials),
         out_shape=jax.ShapeDtypeStruct((WIDTHS, span), jnp.float32),
-        in_specs=[pl.BlockSpec(memory_space=pl.ANY)] * 3,
+        in_specs=[pl.BlockSpec(memory_space=pltpu.HBM)] * 3,
         out_specs=pl.BlockSpec(memory_space=pltpu.VMEM),
         scratch_shapes=[
             pltpu.VMEM((depth, span), spectrogram.dtype),

time: 22.6 us -> 22.6 us (level)
  no operation moved by 1% of the time
where the time goes in v2:
time: 22.6 us; the launch traced here: 22.4 us
  Pallas kernels  19.4 us (86%)
  local copies, waits for them, and re-layouts  2.99 us (13%)
    pallas_call x1, Pallas kernels, shards_one_back(): pl.pallas_call(functools.partial(search, bands, slots, all_trials), out_s...  19.4 us
    unnamed x7, local copies, waits for them, and re-layouts  2.99 us

profile of v2, /device:TPU:0, one launch (start us, length us, event | category | flops | bytes accessed | tf_op | source)
XLA Modules:
  0.0 22.4 jit_solution(6893195030392570494)
XLA Ops:
  0.0 0.0 copy-start
  0.0 1.0 %copy-done = bf16[512,512]{1,0:T(8,128)(2,1)S(1)} copy-done((bf16[512,512]{1,0:T(8,128)(2,1)S(1)}, bf16[512,512]{1,0:T(8,128)(2,1)}, u32[]{:S(2)}) %copy-start) | copy-done | bytes 524312
  1.0 0.0 copy-start.1
  1.0 0.7 %copy-done.1 = s32[254]{0:T(256)S(1)} copy-done((s32[254]{0:T(256)S(1)}, s32[254]{0:T(256)}, u32[]{:S(2)}) %copy-start.1) | copy-done | bytes 1040
  1.7 0.0 copy-start.2
  1.7 0.7 %copy-done.2 = s32[127]{0:T(128)S(1)} copy-done((s32[127]{0:T(128)S(1)}, s32[127]{0:T(128)}, u32[]{:S(2)}) %copy-start.2) | copy-done | bytes 532
  2.4 19.4 %shard_map.37 = f32[9,512]{1,0:T(8,128)S(1)} custom-call(bf16[512,512]{1,0:T(8,128)(2,1)S(1)} %copy-done, s32[127]{0:T(128)S(1)} %copy-done.2, s32[254]{0:T(256)S(1)} %copy-done.1), custom_call_target="tpu_custom_call" | custom-call | tf_op jit(solution)/shard_map/pallas_call | solution.py:393
  21.8 0.6 %copy.5 = f32[9,512]{1,0:T(8,128)} copy(f32[9,512]{1,0:T(8,128)S(1)} %shard_map.37) | data formatting | bytes 36864
Async XLA Ops:
  0.0 1.0 %copy-start = (bf16[512,512]{1,0:T(8,128)(2,1)S(1)}, bf16[512,512]{1,0:T(8,128)(2,1)}, u32[]{:S(2)}) copy-start(bf16[512,512]{1,0:T(8,128)(2,1)} %spec_hbm.1) | copy-start | bytes 1572868
  1.0 0.7 %copy-start.1 = (s32[254]{0:T(256)S(1)}, s32[254]{0:T(256)}, u32[]{:S(2)}) copy-start(s32[254]{0:T(256)} %rest_hbm.1) | copy-start | bytes 3052
  1.7 0.7 %copy-start.2 = (s32[127]{0:T(128)S(1)}, s32[127]{0:T(128)}, u32[]{:S(2)}) copy-start(s32[127]{0:T(128)} %share_hbm.1) | copy-start | bytes 1528

commit v3 on v2

--- a/solution.py
+++ b/solution.py
@@ -410,9 +410,7 @@
             pltpu.SemaphoreType.DMA((3,)),
         ]
         + [sems] * 8,
-        compiler_params=pltpu.CompilerParams(
-            collective_id=0, has_side_effects=True, vmem_limit_bytes=16 * 2**20
-        ),
+        compiler_params=pltpu.CompilerParams(collective_id=0, has_side_effects=True),
     )(spectrogram, low_share, jitter)
 
 

time: 22.6 us -> 21.5 us (0.951)
  local copies, waits for them, and re-layouts: 2.99 us -> 1.38 us
  Pallas kernels: 19.4 us -> 19.9 us
    unnamed x7 -> x1, local copies, waits for them, and re-layouts: 2.99 us -> 1.38 us
    pallas_call x1, Pallas kernels: 19.4 us -> 19.9 us  [shards_one_back(): pl.pallas_call(functools.partial(search, bands, slots, all_trials), out_s...]
where the time goes in v3:
time: 21.5 us; the launch traced here: 21.3 us
  Pallas kernels  19.9 us (93%)
  local copies, waits for them, and re-layouts  1.38 us (6%)
    pallas_call x1, Pallas kernels, shards_one_back(): pl.pallas_call(functools.partial(search, bands, slots, all_trials), out_s...  19.9 us
    unnamed x1, local copies, waits for them, and re-layouts  1.38 us

profile of v3, /device:TPU:0, one launch (start us, length us, event | category | flops | bytes accessed | tf_op | source)
XLA Modules:
  0.0 21.3 jit_solution(6942679248362858576)
XLA Ops:
  0.0 19.9 %shard_map.37 = f32[9,512]{1,0:T(8,128)} custom-call(bf16[512,512]{1,0:T(8,128)(2,1)} %spec_hbm.1, s32[127]{0:T(128)} %share_hbm.1, s32[254]{0:T(256)} %rest_hbm.1), custom_call_target="tpu_custom_call" | custom-call | tf_op jit(solution)/shard_map/pallas_call | solution.py:393
  19.9 1.4 %copy.5 = f32[9,512]{1,0:T(8,128)} copy(f32[9,512]{1,0:T(8,128)} %shard_map.37) | data formatting | bytes 36864

commit v4 on v3

--- a/solution.py
+++ b/solution.py
@@ -179,10 +179,10 @@
 
 
 def search(
-    bands, slots, all_trials,
+    bands, slots, all_trials, cuts,
     spec_hbm, share_hbm, rest_hbm, best_ref,
-    spec, share, rest, base_rows, rows, here, before, part, parts, mine, whole,
-    in_sem, here_send, here_recv, next_send, next_recv, part_send, part_recv, all_send, all_recv,
+    spec, share, rest, base_rows, rows, here, before, part, parts,
+    in_sem, here_send, here_recv, next_send, next_recv, part_send, part_recv,
 ):
     k, m = lax.axis_index("freq"), lax.axis_index("tm")
     span = spec.shape[1]
@@ -300,19 +300,36 @@
         state = merged(state, count, k * width, 0, all_trials, share, rest, lane)
         count = count * 2
 
+    def part_copy(j, i):
+        span_rows = pl.ds(cuts[i], cuts[i + 1] - cuts[i])
+        return pltpu.make_async_remote_copy(
+            src_ref=part.at[span_rows], dst_ref=parts.at[k, span_rows],
+            send_sem=part_send.at[i, j], recv_sem=part_recv.at[i, j],
+            device_id=(lax.rem(k + j, bands), m), device_id_type=MESH,
+        )
+
+    def part_arrival(j, i):
+        came = parts.at[lax.rem(k + bands - j, bands), pl.ds(cuts[i], cuts[i + 1] - cuts[i])]
+        return pltpu.make_async_remote_copy(
+            src_ref=came, dst_ref=came, send_sem=part_send.at[i, j], recv_sem=part_recv.at[i, j],
+            device_id=(k, m), device_id_type=MESH,
+        )
+
     window = state[0]
-    flat = 0
-    piece = part.shape[1]
+    sent = 0
+    used = WIDTHS * chunks
+    part[used:] = jnp.zeros((part.shape[0] - used, LANES), jnp.float32)
     for level in range(WIDTHS):
         w = 2**level
         peak = functools.reduce(jnp.maximum, window)[chunks:]
-        peak = peak * (1.0 / math.sqrt(all_trials * SUMMED * w))
-        done = 0
-        while done < chunks:
-            slot = flat % piece
-            take = min(chunks - done, piece - slot)
-            part[flat // piece, slot : slot + take, :] = peak[done : done + take]
-            done, flat = done + take, flat + take
+        part[level * chunks : (level + 1) * chunks] = peak * (
+            1.0 / math.sqrt(all_trials * SUMMED * w)
+        )
+        if (level + 1) * chunks == cuts[sent + 1] or level + 1 == WIDTHS:
+            for j in order:
+                if j > 0:
+                    part_copy(j, sent).start()
+            sent = sent + 1
         if level + 1 < WIDTHS:
             later = []
             for row in window:
@@ -321,55 +338,29 @@
                     above = moved(row, above, w, lane)
                 later.append(row + above)
             window = later
-    while flat < bands * piece:
-        part[flat // piece, flat % piece : flat % piece + 1, :] = jnp.zeros((1, LANES), jnp.float32)
-        flat = flat + 1
-
-    def part_copy(j):
-        to = lax.rem(k + j, bands)
-        return pltpu.make_async_remote_copy(
-            src_ref=part.at[to], dst_ref=parts.at[k],
-            send_sem=part_send.at[j], recv_sem=part_recv.at[j],
-            device_id=(to, m), device_id_type=MESH,
-        )
-
-    def whole_copy(j):
-        to = lax.rem(k + j, bands)
-        return pltpu.make_async_remote_copy(
-            src_ref=mine, dst_ref=whole.at[k],
-            send_sem=all_send.at[j], recv_sem=all_recv.at[j],
-            device_id=(to, m), device_id_type=MESH,
-        )
-
-    for j in order:
-        if j > 0:
-            part_copy(j).start()
-    parts[k] = part[k]
-    for j in range(1, bands):
-        arrival(parts, part_recv, j).wait_recv()
-    mine[...] = functools.reduce(jnp.maximum, [parts[s] for s in range(bands)])
-    for j in order:
-        if j > 0:
-            whole_copy(j).start()
-    whole[k] = mine[...]
     for j in range(1, bands):
         here_copy(j).wait_send()
-        part_copy(j).wait_send()
 
     @pl.when(m < slots - 1)
     def _():
         for j in range(bands):
             next_copy(j).wait_send()
 
-    for j in range(1, bands):
-        arrival(whole, all_recv, j).wait_recv()
-    for flat in range(WIDTHS * chunks):
-        at = flat % chunks * LANES
-        best_ref[flat // chunks : flat // chunks + 1, at : at + LANES] = whole[
-            flat // piece, flat % piece : flat % piece + 1, :
-        ]
-    for j in range(1, bands):
-        whole_copy(j).wait_send()
+    parts[k] = part[...]
+    for i in range(len(cuts) - 1):
+        for j in range(1, bands):
+            part_arrival(j, i).wait_recv()
+        best = functools.reduce(
+            jnp.maximum, [parts[s, cuts[i] : cuts[i + 1]] for s in range(bands)]
+        )
+        for flat in range(cuts[i], min(cuts[i + 1], used)):
+            at = flat % chunks * LANES
+            best_ref[flat // chunks : flat // chunks + 1, at : at + LANES] = best[
+                flat - cuts[i] : flat - cuts[i] + 1
+            ]
+    for i in range(len(cuts) - 1):
+        for j in range(1, bands):
+            part_copy(j, i).wait_send()
 
 
 def one_block_back(mesh, channels, span, all_trials):
@@ -387,11 +378,11 @@
     local = depth // SUMMED
     chunks = span // LANES
     each = local // bands
-    piece = -(-WIDTHS * chunks // bands)
+    cuts = (0, 16, -(-WIDTHS * chunks // SUBLANES) * SUBLANES)
     sems = pltpu.SemaphoreType.DMA((bands,))
     vmem = lambda *shape: pltpu.VMEM(shape, jnp.float32)
     return pl.pallas_call(
-        functools.partial(search, bands, slots, all_trials),
+        functools.partial(search, bands, slots, all_trials, cuts),
         out_shape=jax.ShapeDtypeStruct((WIDTHS, span), jnp.float32),
         in_specs=[pl.BlockSpec(memory_space=pltpu.HBM)] * 3,
         out_specs=pl.BlockSpec(memory_space=pltpu.VMEM),
@@ -403,13 +394,12 @@
             vmem(local, chunks + 1, LANES),
             vmem(bands, each, chunks + 1, LANES),
             vmem(bands, each, chunks + 1, LANES),
-            vmem(bands, piece, LANES),
-            vmem(bands, piece, LANES),
-            vmem(piece, LANES),
-            vmem(bands, piece, LANES),
+            vmem(cuts[-1], LANES),
+            vmem(bands, cuts[-1], LANES),
             pltpu.SemaphoreType.DMA((3,)),
         ]
-        + [sems] * 8,
+        + [sems] * 4
+        + [pltpu.SemaphoreType.DMA((len(cuts) - 1, bands))] * 2,
         compiler_params=pltpu.CompilerParams(collective_id=0, has_side_effects=True),
     )(spectrogram, low_share, jitter)
 

time: 21.5 us -> 20.2 us (0.940)
  Pallas kernels: 19.9 us -> 18.6 us
    pallas_call x1, Pallas kernels: 19.9 us -> 18.6 us  [shards_one_back(): pl.pallas_call(functools.partial(search, bands, slots, all_trials, cuts),...]
where the time goes in v4:
time: 20.2 us; the launch traced here: 20 us
  Pallas kernels  18.6 us (92%)
  local copies, waits for them, and re-layouts  1.38 us (7%)
    pallas_call x1, Pallas kernels, shards_one_back(): pl.pallas_call(functools.partial(search, bands, slots, all_trials, cuts),...  18.6 us
    unnamed x1, local copies, waits for them, and re-layouts  1.38 us

profile of v4, /device:TPU:0, one launch (start us, length us, event | category | flops | bytes accessed | tf_op | source)
XLA Modules:
  0.0 20.0 jit_solution(8565440273025260542)
XLA Ops:
  0.0 18.6 %shard_map.37 = f32[9,512]{1,0:T(8,128)} custom-call(bf16[512,512]{1,0:T(8,128)(2,1)} %spec_hbm.1, s32[127]{0:T(128)} %share_hbm.1, s32[254]{0:T(256)} %rest_hbm.1), custom_call_target="tpu_custom_call" | custom-call | tf_op jit(solution)/shard_map/pallas_call | solution.py:384
  18.6 1.4 %copy.5 = f32[9,512]{1,0:T(8,128)} copy(f32[9,512]{1,0:T(8,128)} %shard_map.37) | data formatting | bytes 36864

commit v5 on v4

--- a/solution.py
+++ b/solution.py
@@ -182,7 +182,7 @@
     bands, slots, all_trials, cuts,
     spec_hbm, share_hbm, rest_hbm, best_ref,
     spec, share, rest, base_rows, rows, here, before, part, parts,
-    in_sem, here_send, here_recv, next_send, next_recv, part_send, part_recv,
+    in_sem, sems, part_sems,
 ):
     k, m = lax.axis_index("freq"), lax.axis_index("tm")
     span = spec.shape[1]
@@ -190,12 +190,18 @@
     local = spec.shape[0] // SUMMED
     each = local // bands
 
-    loads = [
-        pltpu.make_async_copy(spec_hbm, spec, in_sem.at[0]),
-        pltpu.make_async_copy(share_hbm, share, in_sem.at[1]),
-        pltpu.make_async_copy(rest_hbm, rest, in_sem.at[2]),
+    half = local // 2
+    spec_loads = []
+    for i in range(2):
+        channels = pl.ds(i * half * SUMMED, half * SUMMED)
+        spec_loads.append(
+            pltpu.make_async_copy(spec_hbm.at[channels], spec.at[channels], in_sem.at[i])
+        )
+    table_loads = [
+        pltpu.make_async_copy(share_hbm, share, in_sem.at[2]),
+        pltpu.make_async_copy(rest_hbm, rest, in_sem.at[3]),
     ]
-    for load in loads:
+    for load in spec_loads + table_loads:
         load.start()
 
     barrier = pltpu.get_barrier_semaphore()
@@ -218,15 +224,20 @@
     def _():
         before[...] = jnp.zeros_like(before)
 
-    for load in loads:
+    row_of = lax.broadcasted_iota(jnp.int32, (half, half * SUMMED), 0)
+    channel = lax.broadcasted_iota(jnp.int32, (half, half * SUMMED), 1)
+    ones = jnp.where(channel // SUMMED == row_of, 1.0, 0.0).astype(jnp.bfloat16)
+    for i in range(2):
+        spec_loads[i].wait()
+        base = jnp.dot(
+            ones,
+            spec[i * half * SUMMED : (i + 1) * half * SUMMED],
+            preferred_element_type=jnp.float32,
+        )
+        for q in range(chunks):
+            base_rows[i * half : (i + 1) * half, q, :] = base[:, q * LANES : (q + 1) * LANES]
+    for load in table_loads:
         load.wait()
-
-    row_of = lax.broadcasted_iota(jnp.int32, (local, local * SUMMED), 0)
-    channel = lax.broadcasted_iota(jnp.int32, (local, local * SUMMED), 1)
-    ones = jnp.where(channel // SUMMED == row_of, 1.0, 0.0).astype(jnp.bfloat16)
-    base = jnp.dot(ones, spec[...], preferred_element_type=jnp.float32)
-    for q in range(chunks):
-        base_rows[:, q, :] = base[:, q * LANES : (q + 1) * LANES]
     state = [[base_rows[s]] for s in range(local)]
     count = 2
     while count <= local:
@@ -247,7 +258,7 @@
         to = lax.rem(k + j, bands)
         return pltpu.make_async_remote_copy(
             src_ref=rows.at[pl.ds(to * each, each)], dst_ref=here.at[k],
-            send_sem=here_send.at[j], recv_sem=here_recv.at[j],
+            send_sem=sems.at[0], recv_sem=sems.at[1],
             device_id=(to, m), device_id_type=MESH,
         )
 
@@ -255,17 +266,17 @@
         to = lax.rem(k + j, bands)
         return pltpu.make_async_remote_copy(
             src_ref=rows.at[pl.ds(to * each, each)], dst_ref=before.at[k],
-            send_sem=next_send.at[j], recv_sem=next_recv.at[j],
+            send_sem=sems.at[2], recv_sem=sems.at[3],
             device_id=(to, m + 1), device_id_type=MESH,
         )
 
-    def arrival(buffer, sems, j):
-        came = buffer.at[lax.rem(k + bands - j, bands)]
+    def all_of(blocks, sem):
         return pltpu.make_async_remote_copy(
-            src_ref=came, dst_ref=came, send_sem=sems.at[j], recv_sem=sems.at[j],
+            src_ref=blocks, dst_ref=blocks, send_sem=sem, recv_sem=sem,
             device_id=(k, m), device_id_type=MESH,
         )
 
+    others = pl.ds(0, bands - 1)
     order = sorted(range(bands), key=lambda j: -min(j, bands - j))
 
     @pl.when(m < slots - 1)
@@ -278,13 +289,11 @@
             here_copy(j).start()
     here[k] = rows[pl.ds(k * each, each)]
 
-    for j in range(1, bands):
-        arrival(here, here_recv, j).wait_recv()
+    all_of(here.at[others], sems.at[1]).wait_recv()
 
     @pl.when(m > 0)
     def _():
-        for j in range(bands):
-            arrival(before, next_recv, j).wait_recv()
+        all_of(before, sems.at[3]).wait_recv()
 
     state = []
     for s in range(bands):
@@ -304,16 +313,12 @@
         span_rows = pl.ds(cuts[i], cuts[i + 1] - cuts[i])
         return pltpu.make_async_remote_copy(
             src_ref=part.at[span_rows], dst_ref=parts.at[k, span_rows],
-            send_sem=part_send.at[i, j], recv_sem=part_recv.at[i, j],
+            send_sem=part_sems.at[0, i], recv_sem=part_sems.at[1, i],
             device_id=(lax.rem(k + j, bands), m), device_id_type=MESH,
         )
 
-    def part_arrival(j, i):
-        came = parts.at[lax.rem(k + bands - j, bands), pl.ds(cuts[i], cuts[i + 1] - cuts[i])]
-        return pltpu.make_async_remote_copy(
-            src_ref=came, dst_ref=came, send_sem=part_send.at[i, j], recv_sem=part_recv.at[i, j],
-            device_id=(k, m), device_id_type=MESH,
-        )
+    def part_of_others(i):
+        return parts.at[others, pl.ds(cuts[i], cuts[i + 1] - cuts[i])]
 
     window = state[0]
     sent = 0
@@ -338,18 +343,15 @@
                     above = moved(row, above, w, lane)
                 later.append(row + above)
             window = later
-    for j in range(1, bands):
-        here_copy(j).wait_send()
+    all_of(here.at[others], sems.at[0]).wait_send()
 
     @pl.when(m < slots - 1)
     def _():
-        for j in range(bands):
-            next_copy(j).wait_send()
+        all_of(before, sems.at[2]).wait_send()
 
     parts[k] = part[...]
     for i in range(len(cuts) - 1):
-        for j in range(1, bands):
-            part_arrival(j, i).wait_recv()
+        all_of(part_of_others(i), part_sems.at[1, i]).wait_recv()
         best = functools.reduce(
             jnp.maximum, [parts[s, cuts[i] : cuts[i + 1]] for s in range(bands)]
         )
@@ -359,8 +361,7 @@
                 flat - cuts[i] : flat - cuts[i] + 1
             ]
     for i in range(len(cuts) - 1):
-        for j in range(1, bands):
-            part_copy(j, i).wait_send()
+        all_of(part_of_others(i), part_sems.at[0, i]).wait_send()
 
 
 def one_block_back(mesh, channels, span, all_trials):
@@ -379,7 +380,6 @@
     chunks = span // LANES
     each = local // bands
     cuts = (0, 16, -(-WIDTHS * chunks // SUBLANES) * SUBLANES)
-    sems = pltpu.SemaphoreType.DMA((bands,))
     vmem = lambda *shape: pltpu.VMEM(shape, jnp.float32)
     return pl.pallas_call(
         functools.partial(search, bands, slots, all_trials, cuts),
@@ -396,10 +396,10 @@
             vmem(bands, each, chunks + 1, LANES),
             vmem(cuts[-1], LANES),
             vmem(bands, cuts[-1], LANES),
-            pltpu.SemaphoreType.DMA((3,)),
-        ]
-        + [sems] * 4
-        + [pltpu.SemaphoreType.DMA((len(cuts) - 1, bands))] * 2,
+            pltpu.SemaphoreType.DMA((4,)),
+            pltpu.SemaphoreType.DMA((4,)),
+            pltpu.SemaphoreType.DMA((2, len(cuts) - 1)),
+        ],
         compiler_params=pltpu.CompilerParams(collective_id=0, has_side_effects=True),
     )(spectrogram, low_share, jitter)
 

time: 20.2 us -> 19.6 us (0.970)
  Pallas kernels: 18.6 us -> 18.1 us
    pallas_call x1, Pallas kernels: 18.6 us -> 18.1 us  [shards_one_back(): pl.pallas_call(functools.partial(search, bands, slots, all_trials, cuts),...]
where the time goes in v5:
time: 19.6 us; the launch traced here: 19.4 us
  Pallas kernels  18.1 us (92%)
  local copies, waits for them, and re-layouts  1.38 us (7%)
    pallas_call x1, Pallas kernels, shards_one_back(): pl.pallas_call(functools.partial(search, bands, slots, all_trials, cuts),...  18.1 us
    unnamed x1, local copies, waits for them, and re-layouts  1.38 us

profile of v5, /device:TPU:0, one launch (start us, length us, event | category | flops | bytes accessed | tf_op | source)
XLA Modules:
  0.0 19.4 jit_solution(5505390026346297438)
XLA Ops:
  0.0 18.1 %shard_map.37 = f32[9,512]{1,0:T(8,128)} custom-call(bf16[512,512]{1,0:T(8,128)(2,1)} %spec_hbm.1, s32[127]{0:T(128)} %share_hbm.1, s32[254]{0:T(256)} %rest_hbm.1), custom_call_target="tpu_custom_call" | custom-call | tf_op jit(solution)/shard_map/pallas_call | solution.py:384
  18.1 1.4 %copy.5 = f32[9,512]{1,0:T(8,128)} copy(f32[9,512]{1,0:T(8,128)} %shard_map.37) | data formatting | bytes 36864

commit v6 on v5

--- a/solution.py
+++ b/solution.py
@@ -180,8 +180,8 @@
 
 def search(
     bands, slots, all_trials, cuts,
-    spec_hbm, share_hbm, rest_hbm, best_ref,
-    spec, share, rest, base_rows, rows, here, before, part, parts,
+    spec_hbm, share, rest, best_ref,
+    spec, base_rows, rows, here, before, part, parts,
     in_sem, sems, part_sems,
 ):
     k, m = lax.axis_index("freq"), lax.axis_index("tm")
@@ -197,11 +197,7 @@
         spec_loads.append(
             pltpu.make_async_copy(spec_hbm.at[channels], spec.at[channels], in_sem.at[i])
         )
-    table_loads = [
-        pltpu.make_async_copy(share_hbm, share, in_sem.at[2]),
-        pltpu.make_async_copy(rest_hbm, rest, in_sem.at[3]),
-    ]
-    for load in spec_loads + table_loads:
+    for load in spec_loads:
         load.start()
 
     barrier = pltpu.get_barrier_semaphore()
@@ -236,8 +232,6 @@
         )
         for q in range(chunks):
             base_rows[i * half : (i + 1) * half, q, :] = base[:, q * LANES : (q + 1) * LANES]
-    for load in table_loads:
-        load.wait()
     state = [[base_rows[s]] for s in range(local)]
     count = 2
     while count <= local:
@@ -384,23 +378,24 @@
     return pl.pallas_call(
         functools.partial(search, bands, slots, all_trials, cuts),
         out_shape=jax.ShapeDtypeStruct((WIDTHS, span), jnp.float32),
-        in_specs=[pl.BlockSpec(memory_space=pltpu.HBM)] * 3,
+        in_specs=[pl.BlockSpec(memory_space=pl.ANY)]
+        + [pl.BlockSpec(memory_space=pltpu.SMEM)] * 2,
         out_specs=pl.BlockSpec(memory_space=pltpu.VMEM),
         scratch_shapes=[
             pltpu.VMEM((depth, span), spectrogram.dtype),
-            pltpu.SMEM(low_share.shape, jnp.int32),
-            pltpu.SMEM(jitter.shape, jnp.int32),
             vmem(local, SUBLANES, LANES),
             vmem(local, chunks + 1, LANES),
             vmem(bands, each, chunks + 1, LANES),
             vmem(bands, each, chunks + 1, LANES),
             vmem(cuts[-1], LANES),
             vmem(bands, cuts[-1], LANES),
-            pltpu.SemaphoreType.DMA((4,)),
+            pltpu.SemaphoreType.DMA((2,)),
             pltpu.SemaphoreType.DMA((4,)),
             pltpu.SemaphoreType.DMA((2, len(cuts) - 1)),
         ],
-        compiler_params=pltpu.CompilerParams(collective_id=0, has_side_effects=True),
+        compiler_params=pltpu.CompilerParams(
+            collective_id=0, has_side_effects=True, vmem_limit_bytes=63225856
+        ),
     )(spectrogram, low_share, jitter)
 
 

time: 19.6 us -> 20.3 us (1.036)
  Pallas kernels: 18.1 us -> 18.8 us
    pallas_call x1, Pallas kernels: 18.1 us -> 18.8 us  [shards_one_back(): pl.pallas_call(functools.partial(search, bands, slots, all_trials, cuts),...]
where the time goes in v6:
time: 20.3 us; the launch traced here: 20.1 us
  Pallas kernels  18.8 us (93%)
  local copies, waits for them, and re-layouts  1.38 us (7%)
    pallas_call x1, Pallas kernels, shards_one_back(): pl.pallas_call(functools.partial(search, bands, slots, all_trials, cuts),...  18.8 us
    unnamed x1, local copies, waits for them, and re-layouts  1.38 us

profile of v6, /device:TPU:0, one launch (start us, length us, event | category | flops | bytes accessed | tf_op | source)
XLA Modules:
  0.0 20.1 jit_solution(6925826269717797054)
XLA Ops:
  0.0 18.8 %shard_map.37 = f32[9,512]{1,0:T(8,128)} custom-call(bf16[512,512]{1,0:T(8,128)(2,1)} %spec_hbm.1, s32[127]{0:T(128)} %share.1, s32[254]{0:T(256)} %rest.1), custom_call_target="tpu_custom_call" | custom-call | tf_op jit(solution)/shard_map/pallas_call | solution.py:378
  18.8 1.4 %copy.5 = f32[9,512]{1,0:T(8,128)} copy(f32[9,512]{1,0:T(8,128)} %shard_map.37) | data formatting | bytes 36864

commit v7 on v5

--- a/solution.py
+++ b/solution.py
@@ -164,24 +164,32 @@
     return pltpu.roll(jnp.where(lane >= LANES - delay, above, row), delay, 1)
 
 
-def merged(old, count, first_trial, first_subband, all_trials, share, rest, lane):
+def delays_of(subbands, trials, count, first_trial, first_subband, all_trials, share, rest):
+    jitters = [rest[count - 2 + first_trial + j] for j in range(trials)]
+    delays = []
+    for s in range(subbands):
+        rate = share[all_trials // count - 1 + first_subband + s]
+        delays.append([((first_trial + j) * rate + jitters[j]) >> 6 for j in range(trials)])
+    return delays
+
+
+def merged(old, delays, lane):
     new = []
     for s in range(len(old) // 2):
-        rate = share[all_trials // count - 1 + first_subband + s]
         highs = [(row, pltpu.roll(row, 1, 0)) for row in old[2 * s + 1]]
-        trials = []
-        for j in range(2 * len(highs)):
-            trial = first_trial + j
-            delay = (trial * rate + rest[count - 2 + trial]) >> 6
-            trials.append(old[2 * s][j // 2] + moved(*highs[j // 2], delay, lane))
-        new.append(trials)
+        new.append(
+            [
+                old[2 * s][j // 2] + moved(*highs[j // 2], delays[s][j], lane)
+                for j in range(2 * len(highs))
+            ]
+        )
     return new
 
 
 def search(
     bands, slots, all_trials, cuts,
     spec_hbm, share_hbm, rest_hbm, best_ref,
-    spec, share, rest, base_rows, rows, here, before, part, parts,
+    spec, share, rest, later_delays, base_rows, rows, here, before, part, parts,
     in_sem, sems, part_sems,
 ):
     k, m = lax.axis_index("freq"), lax.axis_index("tm")
@@ -241,7 +249,9 @@
     state = [[base_rows[s]] for s in range(local)]
     count = 2
     while count <= local:
-        state = merged(state, count, 0, k * (local // count), all_trials, share, rest, lane)
+        groups = local // count
+        delays = delays_of(groups, count, count, 0, k * groups, all_trials, share, rest)
+        state = merged(state, delays, lane)
         count = count * 2
     for d in range(local):
         rows[d] = state[0][d][: chunks + 1]
@@ -254,10 +264,12 @@
     def _():
         pl.semaphore_wait(barrier, bands - 1)
 
+    kept = pl.ds(0, chunks)
+
     def here_copy(j):
         to = lax.rem(k + j, bands)
         return pltpu.make_async_remote_copy(
-            src_ref=rows.at[pl.ds(to * each, each)], dst_ref=here.at[k],
+            src_ref=rows.at[pl.ds(to * each, each), kept], dst_ref=here.at[k, :, kept],
             send_sem=sems.at[0], recv_sem=sems.at[1],
             device_id=(to, m), device_id_type=MESH,
         )
@@ -287,9 +299,21 @@
     for j in order:
         if j > 0:
             here_copy(j).start()
-    here[k] = rows[pl.ds(k * each, each)]
-
-    all_of(here.at[others], sems.at[1]).wait_recv()
+    here[k, :, :chunks] = rows[pl.ds(k * each, each), :chunks]
+
+    levels = []
+    width, groups, flat = each, bands, 0
+    while count <= all_trials:
+        width, groups = width * 2, groups // 2
+        level = delays_of(groups, width, count, k * width, 0, all_trials, share, rest)
+        for s in range(groups):
+            for j in range(width):
+                later_delays[flat + s * width + j] = level[s][j]
+        levels.append((groups, width, flat))
+        flat = flat + groups * width
+        count = count * 2
+
+    all_of(here.at[others, :, kept], sems.at[1]).wait_recv()
 
     @pl.when(m > 0)
     def _():
@@ -299,15 +323,13 @@
     for s in range(bands):
         trials = []
         for i in range(each):
-            own, old = here[s, i], before[s, i]
+            own, old = here[s, i, :chunks], before[s, i]
             joint = own[:1] + old[chunks:]
-            trials.append(jnp.concatenate([old[:chunks], joint, own[1:chunks]], axis=0))
+            trials.append(jnp.concatenate([old[:chunks], joint, own[1:]], axis=0))
         state.append(trials)
-    width = each
-    while count <= all_trials:
-        width = width * 2
-        state = merged(state, count, k * width, 0, all_trials, share, rest, lane)
-        count = count * 2
+    for groups, width, flat in levels:
+        delays = [[later_delays[flat + s * width + j] for j in range(width)] for s in range(groups)]
+        state = merged(state, delays, lane)
 
     def part_copy(j, i):
         span_rows = pl.ds(cuts[i], cuts[i + 1] - cuts[i])
@@ -323,7 +345,6 @@
     window = state[0]
     sent = 0
     used = WIDTHS * chunks
-    part[used:] = jnp.zeros((part.shape[0] - used, LANES), jnp.float32)
     for level in range(WIDTHS):
         w = 2**level
         peak = functools.reduce(jnp.maximum, window)[chunks:]
@@ -343,7 +364,7 @@
                     above = moved(row, above, w, lane)
                 later.append(row + above)
             window = later
-    all_of(here.at[others], sems.at[0]).wait_send()
+    all_of(here.at[others, :, kept], sems.at[0]).wait_send()
 
     @pl.when(m < slots - 1)
     def _():
@@ -379,7 +400,7 @@
     local = depth // SUMMED
     chunks = span // LANES
     each = local // bands
-    cuts = (0, 16, -(-WIDTHS * chunks // SUBLANES) * SUBLANES)
+    cuts = (0, 16, WIDTHS * chunks)
     vmem = lambda *shape: pltpu.VMEM(shape, jnp.float32)
     return pl.pallas_call(
         functools.partial(search, bands, slots, all_trials, cuts),
@@ -390,6 +411,7 @@
             pltpu.VMEM((depth, span), spectrogram.dtype),
             pltpu.SMEM(low_share.shape, jnp.int32),
             pltpu.SMEM(jitter.shape, jnp.int32),
+            pltpu.SMEM((all_trials,), jnp.int32),
             vmem(local, SUBLANES, LANES),
             vmem(local, chunks + 1, LANES),
             vmem(bands, each, chunks + 1, LANES),

time: 19.6 us -> 19.2 us (0.980)
  Pallas kernels: 18.1 us -> 17.7 us
    pallas_call x1, Pallas kernels: 18.1 us -> 17.7 us  [shards_one_back(): pl.pallas_call(functools.partial(search, bands, slots, all_trials, cuts),...]
where the time goes in v7:
time: 19.2 us; the launch traced here: 19.1 us
  Pallas kernels  17.7 us (92%)
  local copies, waits for them, and re-layouts  1.38 us (7%)
    pallas_call x1, Pallas kernels, shards_one_back(): pl.pallas_call(functools.partial(search, bands, slots, all_trials, cuts),...  17.7 us
    unnamed x1, local copies, waits for them, and re-layouts  1.38 us

profile of v7, /device:TPU:0, one launch (start us, length us, event | category | flops | bytes accessed | tf_op | source)
XLA Modules:
  0.0 19.1 jit_solution(3570112748480232006)
XLA Ops:
  0.0 17.7 %shard_map.37 = f32[9,512]{1,0:T(8,128)} custom-call(bf16[512,512]{1,0:T(8,128)(2,1)} %spec_hbm.1, s32[127]{0:T(128)} %share_hbm.1, s32[254]{0:T(256)} %rest_hbm.1), custom_call_target="tpu_custom_call" | custom-call | tf_op jit(solution)/shard_map/pallas_call | solution.py:405
  17.7 1.4 %copy.5 = f32[9,512]{1,0:T(8,128)} copy(f32[9,512]{1,0:T(8,128)} %shard_map.37) | data formatting | bytes 36864

commit v8 on v7

--- a/solution.py
+++ b/solution.py
@@ -291,14 +291,15 @@
     others = pl.ds(0, bands - 1)
     order = sorted(range(bands), key=lambda j: -min(j, bands - j))
 
-    @pl.when(m < slots - 1)
-    def _():
-        for j in order:
-            next_copy(j).start()
-
     for j in order:
         if j > 0:
             here_copy(j).start()
+
+    @pl.when(m < slots - 1)
+    def _():
+        for j in order:
+            next_copy(j).start()
+
     here[k, :, :chunks] = rows[pl.ds(k * each, each), :chunks]
 
     levels = []

time: 19.2 us -> 19 us (0.990)
  Pallas kernels: 17.7 us -> 17.4 us
    pallas_call x1, Pallas kernels: 17.7 us -> 17.4 us  [shards_one_back(): pl.pallas_call(functools.partial(search, bands, slots, all_trials, cuts),...]
where the time goes in v8:
time: 19 us; the launch traced here: 18.8 us
  Pallas kernels  17.4 us (92%)
  local copies, waits for them, and re-layouts  1.38 us (7%)
    pallas_call x1, Pallas kernels, shards_one_back(): pl.pallas_call(functools.partial(search, bands, slots, all_trials, cuts),...  17.4 us
    unnamed x1, local copies, waits for them, and re-layouts  1.38 us

profile of v8, /device:TPU:0, one launch (start us, length us, event | category | flops | bytes accessed | tf_op | source)
XLA Modules:
  0.0 18.8 jit_solution(9996039793725303601)
XLA Ops:
  0.0 17.4 %shard_map.37 = f32[9,512]{1,0:T(8,128)} custom-call(bf16[512,512]{1,0:T(8,128)(2,1)} %spec_hbm.1, s32[127]{0:T(128)} %share_hbm.1, s32[254]{0:T(256)} %rest_hbm.1), custom_call_target="tpu_custom_call" | custom-call | tf_op jit(solution)/shard_map/pallas_call | solution.py:406
  17.4 1.4 %copy.5 = f32[9,512]{1,0:T(8,128)} copy(f32[9,512]{1,0:T(8,128)} %shard_map.37) | data formatting | bytes 36864

commit v9 on v8

--- a/solution.py
+++ b/solution.py
@@ -401,7 +401,7 @@
     local = depth // SUMMED
     chunks = span // LANES
     each = local // bands
-    cuts = (0, 16, WIDTHS * chunks)
+    cuts = (0, WIDTHS * chunks)
     vmem = lambda *shape: pltpu.VMEM(shape, jnp.float32)
     return pl.pallas_call(
         functools.partial(search, bands, slots, all_trials, cuts),

time: 19 us -> 19.2 us (1.011)
  Pallas kernels: 17.4 us -> 17.6 us
    pallas_call x1, Pallas kernels: 17.4 us -> 17.6 us  [shards_one_back(): pl.pallas_call(functools.partial(search, bands, slots, all_trials, cuts),...]
where the time goes in v9:
time: 19.2 us; the launch traced here: 19 us
  Pallas kernels  17.6 us (92%)
  local copies, waits for them, and re-layouts  1.38 us (7%)
    pallas_call x1, Pallas kernels, shards_one_back(): pl.pallas_call(functools.partial(search, bands, slots, all_trials, cuts),...  17.6 us
    unnamed x1, local copies, waits for them, and re-layouts  1.38 us

profile of v9, /device:TPU:0, one launch (start us, length us, event | category | flops | bytes accessed | tf_op | source)
XLA Modules:
  0.0 19.0 jit_solution(11785855696167919946)
XLA Ops:
  0.0 17.6 %shard_map.37 = f32[9,512]{1,0:T(8,128)} custom-call(bf16[512,512]{1,0:T(8,128)(2,1)} %spec_hbm.1, s32[127]{0:T(128)} %share_hbm.1, s32[254]{0:T(256)} %rest_hbm.1), custom_call_target="tpu_custom_call" | custom-call | tf_op jit(solution)/shard_map/pallas_call | solution.py:406
  17.6 1.4 %copy.5 = f32[9,512]{1,0:T(8,128)} copy(f32[9,512]{1,0:T(8,128)} %shard_map.37) | data formatting | bytes 36864
